TPU v7x, 256 devices: a whole 4x4x8 slice. The times are simulated.
256 devices in a mesh: copy: 2 (over x_lo), dp: 128 (over x_hi, z, y, core).
Axes of the slice: x: 4 (x_hi: 2, x_lo: 2; x = x_hi * 2 + x_lo), y: 4, z: 8, core: 2. Of those that a mesh axis runs over, the one named last changes fastest.
Arguments:
- features: bfloat16 [2, 49152, 1024], P('copy', 'dp'), may hold values from -100 to 100
- labels: int32 [49152], P('dp'), may hold values from 0 to 5119
- weight: bfloat16 [2, 1024, 5120], P('copy'), may hold values from -0.1875 to 0.1875
Outputs:
- update: float32 [2, 1024, 5120], P('copy', 'dp')
- loss: float32 [2], P('copy')
All inputs are finite; a program needn't handle non-finite values.
Results may differ from a plain program's by a relative error of at most 0.0018.
Values may be sent and summed in bfloat16 or wider, within the bound.
A program may use at most 192 MiB of HBM per device.

v0:
```python
import jax
import jax.numpy as jnp
from jax import lax
from jax.sharding import PartitionSpec as P

temper = 2.0
blend = 0.5
trust = 32.0
decay = 5e-05


def from_partner(value, axis, distance):
    mask = 2**distance
    pairs = [(source, source ^ mask) for source in range(lax.axis_size(axis))]
    return lax.ppermute(value, axis, pairs)


def on_device(features, labels, weight):
    feats = features[0]
    wide = weight[0]
    rows = feats.shape[1] // lax.axis_size("dp")
    images = feats.shape[0] * lax.axis_size("dp")
    classes = jnp.arange(wide.shape[1], dtype=jnp.int32)
    onehot = (labels[:, None] == classes[None, :]).astype(jnp.float32)
    logits = jnp.dot(feats, wide, preferred_element_type=jnp.float32)
    scaled = logits / temper
    soft = jax.nn.softmax(scaled, axis=-1)
    probs = jax.nn.softmax(logits, axis=-1)
    teacher = soft.astype(jnp.bfloat16)
    hard = jax.nn.logsumexp(logits, axis=-1) - jnp.sum(logits * onehot, axis=-1)
    scaled_total = jax.nn.logsumexp(scaled, axis=-1)
    other = from_partner(teacher, "copy", 0).astype(jnp.float32)
    grad_logits = ((1.0 - blend) * (probs - onehot) + blend * temper * (soft - other)).astype(
        jnp.bfloat16
    )
    grad_rows = lax.psum_scatter(
        lax.dot_general(
            feats, grad_logits, (((0,), (0,)), ((), ())), preferred_element_type=jnp.float32
        ),
        "dp",
        scatter_dimension=0,
        tiled=True,
    )
    distil = scaled_total - jnp.sum(other * scaled, axis=-1)
    local_loss = jnp.sum((1.0 - blend) * hard + blend * temper * temper * distil)
    grad_rows = grad_rows / images
    loss_sum = lax.psum(local_loss, "dp")
    square_sum = lax.psum(jnp.sum(grad_rows * grad_rows), "dp")
    wide_f = wide.astype(jnp.float32)
    wnorm = jnp.sqrt(jnp.sum(wide_f * wide_f))
    gnorm = jnp.sqrt(square_sum)
    own_weight = lax.dynamic_slice_in_dim(wide_f, lax.axis_index("dp") * rows, rows, 0)
    update = trust * wnorm / (gnorm + decay * wnorm) * (grad_rows + decay * own_weight)
    loss = (loss_sum / images).reshape(1)
    return (update[None], loss)


def solution(mesh):
    placed = (P("copy", "dp", None), P("dp"), P("copy", None, None))
    return jax.shard_map(
        on_device,
        mesh=mesh,
        in_specs=placed,
        out_specs=(P("copy", "dp", None), P("copy")),
        check_vma=False,
    )
```

profile of v0, /device:TPU:1, one launch (start us, length us, event | category | flops | bytes accessed | tf_op | source)
XLA Modules:
  0.0 1189.6 jit_solution(5728251021051037617)
XLA Ops:
  7.2 0.0 copy-start
  7.2 0.0 copy-start.4
  7.2 0.0 reduce-scatter.4.cloned.1.call-start
  7.2 1.1 copy-done
  8.3 7.1 fusion.19
  15.5 0.0 copy-start.2
  15.5 0.0 copy-done.4
  15.5 8.0 exponential_reduce_fusion.1
  23.5 1.8 fusion.8
  25.3 2.1 collective-permute-start
  27.5 83.3 %collective-permute-done = bf16[384,5120]{1,0:T(8,128)(2,1)S(1)} collective-permute-done((bf16[384,5120]{1,0:T(8,128)(2,1)S(1)}, bf16[384,5120]{1,0:T(8,128)(2,1)S(1)}, u32[]{:S(2)}, u32[]{:S(2)}) %collective-permute-start) | collective-permute-done | bytes 3932192 | tf_op jit(solution)/shard_map/ppermute | solution.py:15
  110.8 0.0 copy-start.3
  110.8 0.0 copy-done.2
  110.8 2.0 copy-done.3
  112.8 13.3 %convolution_bitcast_fusion = f32[1024,5120]{0,1:T(8,128)} fusion(bf16[384,5120]{1,0:T(8,128)(2,1)S(1)} %collective-permute-done, f32[384,5120]{1,0:T(8,128)S(1)} %get-tuple-element.15, f32[384]{0:T(512)S(1)} %get-tuple-element.7, f32[384]{0:T(512)S(1)} %get-tuple-element.12, s32[384]{0:T(512)S(1)} %copy-done.4, f32[384]{0:T(512)S(1)} %get-tuple-element.10, ...), kind=kOutput, calls=%fused_computation.1 | convolution fusion | flops 4052090880 | bytes 33562112 | tf_op jit(solution)/shard_map/dot_general | solution.py:37
  126.1 19.9 %copy.9 = f32[1024,5120]{1,0:T(8,128)} copy(f32[1024,5120]{0,1:T(8,128)} %convolution_bitcast_fusion) | data formatting | bytes 41943040
  146.0 0.0 reduce-scatter.4.cloned.1.call-update
  146.1 14.4 %copy.7 = bf16[1,1024,5120]{1,2,0:T(8,128)(2,1)} copy(bf16[1,1024,5120]{2,1,0:T(8,128)(2,1)} %param.5) | data formatting | bytes 20971520 | tf_op args[2]
  160.5 10.1 multiply_reduce_fusion
  171.3 13.8 %bitcast_convert_fusion = f32[1024,5120]{0,1:T(8,128)} fusion(bf16[1,1024,5120]{1,2,0:T(8,128)(2,1)} %copy.7), kind=kLoop, calls=%fused_computation.4 | loop fusion | flops 5242880 | bytes 31457280 | tf_op jit(solution)/shard_map/convert_element_type | solution.py:49
  185.1 5.6 fusion.4
  190.7 0.0 copy-start.1
  190.7 0.6 add_reduce_fusion
  191.3 647.1 %reduce-scatter.4.cloned.1.call-done = f32[8,5120]{1,0:T(8,128)} async-done(((f32[1024,5120]{1,0:T(8,128)}), f32[8,5120]{1,0:T(8,128)}) %reduce-scatter.4.cloned.1.call-update) | async-done | bytes 163856
  838.5 1.6 copy.10
  840.1 1.3 multiply_reduce_fusion.2
  841.4 331.8 %all-reduce = (f32[]{:T(128)}, f32[]{:T(128)}) all-reduce(f32[]{:T(128)} %multiply_reduce_fusion.2, f32[]{:T(128)} %add_reduce_fusion), channel_id=1, replica_groups=mesh['copy'=2,'dp'=128] {'dp'}, use_global_device_ids=true, to_apply=%region_7.0 | all-reduce | flops 2 | bytes 16 | tf_op jit(solution)/shard_map/psum | solution.py:48
  1173.9 4.0 multiply_bitcast_fusion
  1178.0 3.1 copy.8
  1181.6 0.0 copy-done.1
  (1 shorter events, 0.0 us)
Async XLA Ops:
  7.2 1.1 copy-start
  7.2 8.3 copy-start.4
  7.2 831.3 %reduce-scatter.4.cloned.1.call-start = ((), (), s32[]{:S(2)}) async-start(), calls=%async_computation.1 | async-start | bytes 21135360
  15.5 95.4 %copy-start.2 = (f32[384,5120]{1,0:T(8,128)}, f32[384,5120]{1,0:T(8,128)S(1)}, u32[]{:S(2)}) copy-start(f32[384,5120]{1,0:T(8,128)S(1)} %get-tuple-element.15) | copy-start | bytes 23592964
  25.3 85.5 %collective-permute-start = (bf16[384,5120]{1,0:T(8,128)(2,1)S(1)}, bf16[384,5120]{1,0:T(8,128)(2,1)S(1)}, u32[]{:S(2)}, u32[]{:S(2)}) collective-permute-start(bf16[384,5120]{1,0:T(8,128)(2,1)S(1)} %fusion.8), channel_id=1, source_target_pairs={{0,128},{128,0},{1,129},{129,1},{2,130},{130,2},{3,131},{131,3},{4... | collective-permute-start | bytes 11796488 | tf_op jit(solution)/shard_map/ppermute | solution.py:15
  110.8 2.0 copy-start.3
  190.7 990.9 %copy-start.1 = (bf16[1,384,1024]{2,1,0:T(8,128)(2,1)S(1)}, bf16[1,384,1024]{2,1,0:T(8,128)(2,1)}, u32[]{:S(2)}) copy-start(bf16[1,384,1024]{2,1,0:T(8,128)(2,1)} %param.3) | copy-start | bytes 2359300
Sparse Core Ops, SparseCore 0:
  146.2 692.2 reduce-scatter.3
where the time goes:
time: 1190 us
  waiting for transfers between devices  730 us (61%)
  blocking collectives  332 us (28%)
  other arithmetic  45.3 us (4%)
  local copies, waits for them, and re-layouts  42.2 us (4%)
  matrix products  20.4 us (2%)
  between operations  17.2 us (1%)
    unnamed x2, waiting for transfers between devices  647 us
    psum x1, blocking collectives, on_device(): square_sum = lax.psum(jnp.sum(grad_rows * grad_rows), 'dp')  332 us
    ppermute x1, waiting for transfers between devices, from_partner(): return lax.ppermute(value, axis, pairs)  83.3 us
    unnamed x14, local copies, waits for them, and re-layouts  42.2 us
  transfers between devices with their start and end apart: 2, of which 2 were waited for; matrix products, arithmetic and copies ran while one was open for 4% of the time, Pallas kernels for 0%

commit v1 on v0

v1 whole, which is shorter than its diff:
```python
import functools

import jax
import jax.numpy as jnp
from jax import lax
from jax.experimental import pallas as pl
from jax.experimental.pallas import tpu as pltpu
from jax.sharding import PartitionSpec as P

MESH = pl.DeviceIdType.MESH
NZ, NY = 8, 4
IMG = 384
D = 1024
CLASSES = 5120
SL = CLASSES // 8
IMAGES = 49152
HALF = IMG // 2
GI = 2 * IMG
trust = 32.0
decay = 5e-05
F32, BF16 = jnp.float32, jnp.bfloat16


def fold_lanes(v):
    out = v[:, 0:128]
    for k in range(1, SL // 128):
        out = out + v[:, k * 128 : (k + 1) * 128]
    return out


def fold_rows(v):
    out = v[0:8]
    for k in range(1, v.shape[0] // 8):
        out = out + v[k * 8 : (k + 1) * 8]
    return out


def kernel(
    f_in, w_in, lab_in,
    out_ref, loss_ref,
    F, FT, WS, W16, LAB, LABC, X, G, ACC, STR, COLT, LA, LS, TB, GB,
    SCZ, SCY, SCX,
    S00, R00, S01, R01, S10, R10, S11, R11,
    loc_sem, fs, fr, ws, wr, ls, lr, ss, sr, as_, ar,
    zs, zr, ys, yr, xs, xr,
    s00s, s00r, s01s, s01r, s10s, s10r, s11s, s11r,
):
    cp = lax.axis_index("copy")
    dp = lax.axis_index("dp")
    core = lax.rem(dp, 2)
    y = lax.rem(dp // 2, NY)
    z = lax.rem(dp // (2 * NY), NZ)
    xh = dp // (2 * NY * NZ)
    oc, ox, ok = 1 - cp, 1 - xh, 1 - core

    def dev(c, h, zz, yy, k):
        return (c, ((h * NZ + zz) * NY + yy) * 2 + k)

    partner = dev(oc, xh, z, y, core)
    nonp = dev(oc, ox, z, y, core)
    sib = dev(cp, xh, z, y, ok)

    def flip(v, bit):
        return 1 - v if bit else v

    group = [(a, b, c) for a in range(2) for b in range(2) for c in range(2)][1:]

    def peer(abc):
        a, b, c = abc
        return dev(flip(cp, a), flip(xh, b), z, y, flip(core, c))

    def slot(abc):
        return abc[0] * 4 + abc[1] * 2 + abc[2]

    def ypeer(o):
        return dev(cp, xh, z, lax.rem(y + o, NY), core)

    def zpeer(o):
        return dev(cp, xh, lax.rem(z + o, NZ), y, core)

    def slice_of(c, h, k):
        return pl.ds(pl.multiple_of(((c * 2 + h) * 2 + k) * SL, 128), SL)

    my_s = slice_of(cp, xh, core)

    def block(h, k, lo, rows):
        return pl.ds(pl.multiple_of((h * 2 + k) * HALF + lo, 16), rows)

    loc = [
        pltpu.make_async_copy(
            f_in.at[pl.ds(b * HALF, HALF)], F.at[0, b, block(xh, core, 0, HALF)], loc_sem.at[b]
        )
        for b in range(2)
    ] + [
        pltpu.make_async_copy(w_in.at[:, my_s], WS.at[0], loc_sem.at[2]),
        pltpu.make_async_copy(
            w_in.at[pl.ds(pl.multiple_of((dp // 2) * 16, 16), 16), :], W16, loc_sem.at[3]
        ),
        pltpu.make_async_copy(lab_in, LAB.at[xh, core], loc_sem.at[4]),
    ]
    for c in loc:
        c.start()

    peers = [peer(g) for g in group] + [ypeer(o) for o in range(1, NY)] + [zpeer(o) for o in range(1, NZ)]
    barrier = pltpu.get_barrier_semaphore()
    for p in peers:
        pl.semaphore_signal(barrier, inc=1, device_id=p, device_id_type=MESH)
    pl.semaphore_wait(barrier, len(peers))

    sends = []

    def remote(src, dst, s, r, to):
        c = pltpu.make_async_remote_copy(
            src_ref=src, dst_ref=dst, send_sem=s, recv_sem=r, device_id=to, device_id_type=MESH
        )
        return c

    def push(src, dst, s, r, to):
        c = remote(src, dst, s, r, to)
        c.start()
        sends.append(c)

    def arrive(ref, s, r):
        remote(ref, ref, s, r, partner).wait_recv()

    def quarter(yy, h):
        return pl.ds(pl.multiple_of((yy * 2 + h) * (D // NY // 2), 64), D // NY // 2)

    push(w_in.at[quarter(y, 0), slice_of(oc, xh, core)], WS.at[1, quarter(y, 0)], ws.at[0], wr.at[0], partner)
    push(w_in.at[quarter(y, 1), slice_of(oc, ox, core)], WS.at[1, quarter(y, 1)], ws.at[1], wr.at[1], nonp)

    PART = HALF // 2
    LO, HI = 0, PART

    def fpush(b, kind, own, i, h, k, lo, rows, to, src_i=None):
        at = block(h, k, lo, rows)
        src = f_in.at[pl.ds(b * HALF + lo, rows)] if own else F.at[i if src_i is None else src_i, b, at]
        push(src, F.at[i, b, at], fs.at[b, kind], fr.at[b, kind], to)

    def fwait(b, kind, i, h, k, lo, rows=PART):
        arrive(F.at[i, b, block(h, k, lo, rows)], fs.at[b, kind], fr.at[b, kind])

    def own_to_neighbours(b):
        fpush(b, 0, True, 1, xh, core, LO, PART, partner)
        fpush(b, 2, True, 1, xh, core, HI, PART, nonp)
        fpush(b, 1, True, 1, xh, core, HI, PART, partner)
        fpush(b, 3, True, 1, xh, core, LO, PART, nonp)

    def pass_on(b):
        fwait(b, 0, 1, xh, core, LO)
        fpush(b, 5, False, 0, xh, core, LO, PART, nonp, 1)
        fwait(b, 2, 1, ox, core, HI)
        fpush(b, 6, False, 0, ox, core, HI, PART, partner, 1)
        fpush(b, 7, False, 1, xh, core, LO, PART, sib)
        fpush(b, 9, False, 1, ox, core, HI, PART, sib)

    def share_rest(b):
        fwait(b, 1, 1, xh, core, HI)
        fpush(b, 8, False, 1, xh, core, HI, PART, sib)
        fwait(b, 3, 1, ox, core, LO)
        fpush(b, 10, False, 1, ox, core, LO, PART, sib)

    def share_far(b):
        fwait(b, 5, 0, ox, core, LO)
        fpush(b, 11, False, 0, ox, core, LO, PART, sib)
        fwait(b, 6, 0, ox, core, HI)
        fpush(b, 12, False, 0, ox, core, HI, PART, sib)

    def shared_neighbours(b):
        fwait(b, 7, 1, xh, ok, LO)
        fwait(b, 9, 1, ox, ok, HI)
        fwait(b, 8, 1, xh, ok, HI)
        fwait(b, 10, 1, ox, ok, LO)

    def shared_far(b):
        fwait(b, 11, 0, ox, ok, LO)
        fwait(b, 12, 0, ox, ok, HI)

    own_to_neighbours(0)
    for b in range(2):
        fpush(b, 4, True, 0, xh, core, 0, HALF, sib)

    lab_kinds = [(0, 0, 1), (0, 1, 0), (0, 1, 1)]
    for n, g in enumerate(lab_kinds):
        push(lab_in, LAB.at[xh, core], ls.at[n], lr.at[n], peer(g))

    def logits(i, b, h):
        rows = pl.ds(pl.multiple_of(h * IMG, 128), IMG)
        X[i, b, rows, :] = jnp.dot(F[i, b, rows, :], WS[i], preferred_element_type=F32)

        def body(t, carry):
            at = pl.ds(pl.multiple_of(h * IMG + t * 128, 128), 128)
            lg = X[i, b, at, :]
            m = jnp.max(lg, axis=1, keepdims=True)
            e = jnp.exp(0.5 * (lg - m))
            s = jnp.sum(e, axis=1, keepdims=True)
            s2 = jnp.sum(e * e, axis=1, keepdims=True)
            lane = lax.broadcasted_iota(jnp.int32, (128, 128), 1)
            tile = jnp.where(lane == 0, m, jnp.where(lane == 1, s, s2))
            STR[0, b, 4 * i : 4 * i + 4, at] = tile.T[0:4]
            return carry

        lax.fori_loop(0, IMG // 128, body, 0)

    def transpose(i, b, h):
        def body(t, carry):
            at = pl.ds(pl.multiple_of(h * IMG + t * 128, 128), 128)
            v = F[i, b, at, :].T
            for hh in range(2):
                for zz in range(NZ):
                    for yy in range(NY):
                        g = (hh * NZ + zz) * NY + yy
                        to = ((zz * NY + yy) if i == 0 else (yy * NZ + zz)) * 2 + hh
                        FT[i, b, to * 16 : to * 16 + 16, at] = v[g * 16 : g * 16 + 16]
            return carry

        lax.fori_loop(0, IMG // 128, body, 0)

    def label_columns():
        for h in range(2):
            for k in range(2):
                rows = jnp.concatenate(
                    [
                        jnp.broadcast_to(LAB[h, k, 0:1, t * 128 : t * 128 + 128], (128, 128)).T
                        for t in range(IMG // 128)
                    ],
                    axis=0,
                )
                for b in range(2):
                    o = (h * 2 + k) * HALF
                    LABC[b, o : o + HALF, :] = rows[b * HALF : b * HALF + HALF]

    def send_stats(b):
        for n, g in enumerate(group):
            push(STR.at[0, b], STR.at[slot(g), b], ss.at[b, n], sr.at[b, n], peer(g))

    def wait_stats(b):
        for n, g in enumerate(group):
            arrive(STR.at[slot(g), b], ss.at[b, n], sr.at[b, n])

    base = ((cp * 2 + xh) * 2 + core) * SL

    def combine(b):
        rows = []
        for i in range(2):
            vs = []
            for a in range(2):
                for n in range(4):
                    o = 4 * (i ^ a)
                    vs.append(STR[a * 4 + n, b, o : o + 4, :])
            m = functools.reduce(jnp.maximum, [v[0:1] for v in vs])
            s = s2 = 0.0
            for v in vs:
                e = jnp.exp(0.5 * (v[0:1] - m))
                s = s + v[1:2] * e
                s2 = s2 + v[2:3] * (e * e)
            per_image = (0.5 * jnp.log(s2) + 2.0 * jnp.log(s)) * 0.125
            LS[i, :, :] = LS[i] + jnp.broadcast_to(
                functools.reduce(
                    lambda p, q: p + q, [per_image[:, k * 128 : (k + 1) * 128] for k in range(GI // 128)]
                ),
                (8, 128),
            )
            rows += [m, 1.0 / s, 1.0 / s2]
        pack = jnp.concatenate(rows + rows[:2], axis=0)
        for k in range(GI // 128):
            part = pack[:, k * 128 : (k + 1) * 128]
            part = jnp.concatenate([part, jnp.zeros((120, 128), F32)], axis=0)
            COLT[k * 128 : (k + 1) * 128, :] = part.T

    R = 32

    def finish(b):
        def body(t, carry):
            at = pl.ds(pl.multiple_of(t * R, R), R)
            c = COLT[at, :]
            cls = (lax.broadcasted_iota(jnp.int32, (R, SL), 1) + base).astype(F32)
            oh = cls == LABC[b, at, 0:1]
            x0 = X[0, b, at, :] - c[:, 0:1]
            x1 = X[1, b, at, :] - c[:, 3:4]
            e0 = jnp.exp(0.5 * x0)
            e1 = jnp.exp(0.5 * x1)
            s0 = e0 * c[:, 1:2]
            s1 = e1 * c[:, 4:5]
            q0 = s0.astype(BF16).astype(F32)
            q1 = s1.astype(BF16).astype(F32)
            p0 = e0 * e0 * c[:, 2:3]
            p1 = e1 * e1 * c[:, 5:6]
            hot = jnp.where(oh, 0.5, 0.0)
            G[0, at, :] = (0.5 * p0 - hot + (s0 - q1)).astype(BF16)
            G[1, at, :] = (0.5 * p1 - hot + (s1 - q0)).astype(BF16)
            l0 = fold_lanes((q1 + hot) * x0) - c[:, 0:1] * fold_lanes(s1 - q1)
            l1 = fold_lanes((q0 + hot) * x1) - c[:, 3:4] * fold_lanes(s0 - q0)
            LA[0, :, :] = LA[0] + fold_rows(l0)
            LA[1, :, :] = LA[1] + fold_rows(l1)
            return carry

        lax.fori_loop(0, GI // R, body, 0)

    def wgrad(i, b, start, count, rows, first):
        def body(t, carry):
            j = lax.rem(start + t, D // rows)
            at = pl.ds(pl.multiple_of(j * rows, rows), rows)
            d = jnp.dot(FT[i, b, at, :], G[i], preferred_element_type=F32)
            ACC[i, at, :] = d if first else ACC[i, at, :] + d
            return carry

        lax.fori_loop(0, count, body, 0)

    LA[...] = jnp.zeros_like(LA)
    LS[...] = jnp.zeros_like(LS)

    def wsend(kind, yy, half, o):
        push(WS.at[1, quarter(yy, half)], WS.at[1, quarter(yy, half)], ws.at[kind], wr.at[kind], ypeer(o))

    def wwait(kind, yy, half):
        arrive(WS.at[1, quarter(yy, half)], ws.at[kind], wr.at[kind])

    yd, yu, yo = lax.rem(y + NY - 1, NY), lax.rem(y + 1, NY), lax.rem(y + 2, NY)

    for c in loc:
        c.wait()
    fwait(0, 4, 0, xh, ok, 0, HALF)
    logits(0, 0, xh)
    wwait(0, y, 0)
    wsend(2, y, 0, 1)
    wwait(1, y, 1)
    wsend(4, y, 1, NY - 1)
    wsend(3, y, 1, 1)
    wsend(5, y, 0, NY - 1)
    pass_on(0)
    own_to_neighbours(1)
    transpose(0, 0, xh)
    fwait(1, 4, 0, xh, ok, 0, HALF)
    wwait(2, yd, 0)
    wsend(6, yd, 0, 1)
    wwait(4, yu, 1)
    wsend(7, yu, 1, NY - 1)
    logits(0, 1, xh)
    share_rest(0)
    transpose(0, 1, xh)
    for n, (_, bb, c) in enumerate(lab_kinds):
        arrive(LAB.at[flip(xh, bb), flip(core, c)], ls.at[n], lr.at[n])
    label_columns()
    wwait(3, yd, 1)
    wwait(5, yu, 0)
    wwait(6, yo, 0)
    wwait(7, yo, 1)
    shared_neighbours(0)
    logits(1, 0, 0)
    share_far(0)
    logits(1, 0, 1)
    shared_far(0)
    logits(0, 0, ox)
    send_stats(0)
    transpose(0, 0, ox)
    pass_on(1)
    transpose(1, 0, 0)
    transpose(1, 0, 1)
    wait_stats(0)
    combine(0)
    finish(0)
    share_rest(1)
    wgrad(0, 0, 0, 4, D // 4, True)
    wgrad(1, 0, 0, 4, D // 4, True)
    shared_neighbours(1)
    logits(1, 1, 0)
    logits(1, 1, 1)
    share_far(1)
    transpose(1, 1, 0)
    transpose(1, 1, 1)
    shared_far(1)
    logits(0, 1, ox)
    send_stats(1)
    transpose(0, 1, ox)
    wait_stats(1)
    combine(1)
    finish(1)

    def ring(n, me, H, chunk, S, RB, ssem, rsem, toward):
        steps = n // 2
        for t in range(steps):
            d = steps - t
            for way in range(2):
                j = lax.rem(me + (n - d if way == 0 else d), n)
                out = S[t]
                if t == 0:
                    out[way, :, :] = chunk(j, way * H, H).astype(out.dtype)
                else:
                    arrive(RB[t - 1].at[way], ssem.at[way, t - 1], rsem.at[way, t - 1])
                    if t == 1:
                        for half in range(2):
                            v = chunk(j, half * H, H)
                            if half == way:
                                v = v + RB[0][way].astype(F32)
                            out[way, half * H : half * H + H, :] = v.astype(out.dtype)
                    else:
                        v = chunk(j, 0, 2 * H) + RB[t - 1][way].astype(F32)
                        out[way, :, :] = v.astype(out.dtype)
                push(out.at[way], RB[t].at[way], ssem.at[way, t], rsem.at[way, t], toward[way])
            yield
        for way in range(2):
            arrive(RB[steps - 1].at[way], ssem.at[way, steps - 1], rsem.at[way, steps - 1])

    ydirs, zdirs = (ypeer(NY - 1), ypeer(1)), (zpeer(NZ - 1), zpeer(1))

    def acc_chunk(i, size):
        def chunk(j, lo, rows):
            return ACC[i, pl.ds(pl.multiple_of(j * size + lo, 16), rows), :]

        return chunk

    c0, c1 = D // NZ, D // NY
    r0 = ring(NZ, z, c0 // 2, acc_chunk(0, c0), S00, R00, s00s, s00r, zdirs)
    r1 = ring(NY, y, c1 // 2, acc_chunk(1, c1), S10, R10, s10s, s10r, ydirs)

    def own0():
        at = pl.ds(pl.multiple_of(z * c0, 16), c0)
        ACC[0, at, :] = ACC[0, at, :] + (R00[-1][0].astype(F32) + R00[-1][1].astype(F32))

    def own1():
        at = pl.ds(pl.multiple_of(y * c1, 16), c1)
        ACC[1, at, :] = ACC[1, at, :] + (R10[-1][0].astype(F32) + R10[-1][1].astype(F32))

    def sub_chunk(i, first):
        def chunk(j, lo, rows):
            return ACC[i, pl.ds(pl.multiple_of(first + j * 32 + lo, 16), rows), :]

        return chunk

    q0 = ring(NY, y, 16, sub_chunk(0, z * c0), S01, R01, s01s, s01r, ydirs)
    q1 = ring(NZ, z, 16, sub_chunk(1, y * c1), S11, R11, s11s, s11r, zdirs)

    def go(gen):
        for _ in gen:
            return

    wgrad(0, 1, z + NZ // 2, 1, c0, False)
    wgrad(1, 1, y + NY // 2, 1, c1, False)
    go(r0)
    go(r1)
    wgrad(0, 1, z + NZ // 2 + 1, NZ - 1, c0, False)
    go(r0)
    wgrad(1, 1, y + NY // 2 + 1, NY - 1, c1, False)
    go(r1)
    go(r0)
    go(r0)
    go(r1)
    own1()
    go(q1)
    go(r0)
    own0()
    go(q0)
    go(q1)
    go(q0)
    go(q1)
    go(q0)
    go(q1)
    go(q1)

    inv = 1.0 / IMAGES
    sq = []
    for i in range(2):
        at = pl.ds(pl.multiple_of(z * c0 + y * 32 if i == 0 else y * c1 + z * 32, 32), 32)
        last = (R01 if i == 0 else R11)[-1]
        v = (ACC[i, at, :] + (last[0].astype(F32) + last[1].astype(F32))) * inv
        TB[i, :, :] = v
        sq.append(fold_rows(fold_lanes(v * v)))
    for n, g in enumerate(group):
        a, b, c = g
        off = pl.ds(pl.multiple_of((flip(xh, b) * 2 + flip(core, c)) * 8, 8), 8)
        push(TB.at[a, off], GB.at[:, my_s], as_.at[n], ar.at[n], peer(g))
    GB[:, my_s] = TB[0, pl.ds(pl.multiple_of((xh * 2 + core) * 8, 8), 8), :]

    vals = []
    for i in range(2):
        wq = 0.0
        for h in range(2):
            at = pl.ds(pl.multiple_of(((h * NZ + z) * NY + y) * 16, 16), 16)
            wv = WS[i, at, :].astype(F32)
            wq = wq + fold_rows(fold_lanes(wv * wv))
        lv = LS[i] * 0.125 - LA[i]
        vals.append([jnp.sum(v, axis=0, keepdims=True) for v in (sq[i], lv, wq)])
    row = lax.broadcasted_iota(jnp.int32, (8, 128), 0)
    tile = jnp.zeros((8, 128), F32)
    for r in range(3):
        v0, v1 = vals[0][r], vals[1][r]
        tile = jnp.where(row == r, jnp.where(cp == 0, v0, v1), tile)
        tile = jnp.where(row == 3 + r, jnp.where(cp == 0, v1, v0), tile)

    SCZ[0, :, :] = tile
    for o in range(1, NZ):
        push(SCZ.at[0], SCZ.at[o], zs.at[o - 1], zr.at[o - 1], zpeer(o))
    for o in range(1, NZ):
        arrive(SCZ.at[o], zs.at[o - 1], zr.at[o - 1])
    SCY[0, :, :] = jnp.sum(SCZ[...], axis=0)
    for o in range(1, NY):
        push(SCY.at[0], SCY.at[o], ys.at[o - 1], yr.at[o - 1], ypeer(o))
    for o in range(1, NY):
        arrive(SCY.at[o], ys.at[o - 1], yr.at[o - 1])
    SCX[0, :, :] = jnp.sum(SCY[...], axis=0)
    for n, g in enumerate(group):
        push(SCX.at[0], SCX.at[slot(g)], xs.at[n], xr.at[n], peer(g))
    for n, g in enumerate(group):
        arrive(SCX.at[slot(g)], xs.at[n], xr.at[n])
    total = jnp.sum(SCX[...], axis=0)
    mine = jnp.where(cp == 0, total[0:3], total[3:6])
    mine = jnp.sum(mine, axis=1, keepdims=True)
    gnorm = jnp.sqrt(mine[0:1])
    wnorm = jnp.sqrt(mine[2:3])
    scale = trust * wnorm / (gnorm + decay * wnorm)
    loss_ref[...] = jnp.broadcast_to(mine[1:2] * inv, (8, 128))

    for n, (a, b, c) in enumerate(group):
        src = slice_of(flip(cp, a), flip(xh, b), flip(core, c))
        arrive(GB.at[:, src], as_.at[n], ar.at[n])
    w16 = W16[...].astype(F32)
    own_w = jnp.where(core == 0, w16[0:8], w16[8:16])
    out_ref[...] = scale * (GB[...] + decay * own_w)

    for c in sends:
        c.wait_send()


def on_device(features, labels, weight):
    lab = jnp.broadcast_to(labels.astype(F32)[None, :], (8, IMG))
    dma = pltpu.SemaphoreType.DMA
    vm = pltpu.VMEM
    any_ = pl.BlockSpec(memory_space=pl.ANY)
    ring_bufs = []
    ring_sems = []
    for rows, types in (
        (D // NZ, [BF16] * (NZ // 2 - 1) + [F32]),
        (32, [F32] * (NY // 2)),
        (D // NY, [BF16] * (NY // 2)),
        (32, [F32] * (NZ // 2)),
    ):
        bufs = tuple(vm((2, rows // 2 if t == 0 else rows, SL), dt) for t, dt in enumerate(types))
        ring_bufs += [bufs, bufs]
        ring_sems += [dma((2, len(types)))] * 2
    update, loss = pl.pallas_call(
        kernel,
        out_shape=(
            jax.ShapeDtypeStruct((8, CLASSES), F32),
            jax.ShapeDtypeStruct((8, 128), F32),
        ),
        in_specs=[any_, any_, any_],
        out_specs=(pl.BlockSpec(memory_space=vm), pl.BlockSpec(memory_space=vm)),
        scratch_shapes=[
            vm((2, 2, GI, D), BF16),
            vm((2, 2, D, GI), BF16),
            vm((2, D, SL), BF16),
            vm((16, CLASSES), BF16),
            vm((2, 2, 8, IMG), F32),
            vm((2, GI, 128), F32),
            vm((2, 2, GI, SL), F32),
            vm((2, GI, SL), BF16),
            vm((2, D, SL), F32),
            vm((8, 2, 8, GI), F32),
            vm((GI, 128), F32),
            vm((2, 8, 128), F32),
            vm((2, 8, 128), F32),
            vm((2, 32, SL), F32),
            vm((8, CLASSES), F32),
            vm((NZ, 8, 128), F32),
            vm((NY, 8, 128), F32),
            vm((8, 8, 128), F32),
            *ring_bufs,
            dma((5,)),
            dma((2, 13)), dma((2, 13)),
            dma((8,)), dma((8,)),
            dma((3,)), dma((3,)),
            dma((2, 7)), dma((2, 7)),
            dma((7,)), dma((7,)),
            dma((NZ - 1,)), dma((NZ - 1,)),
            dma((NY - 1,)), dma((NY - 1,)),
            dma((7,)), dma((7,)),
            *ring_sems,
        ],
        compiler_params=pltpu.CompilerParams(
            collective_id=0, has_side_effects=True, vmem_limit_bytes=56 * 2**20
        ),
    )(features[0], weight[0], lab)
    return (update[None], loss[0, :1])


def solution(mesh):
    placed = (P("copy", "dp", None), P("dp"), P("copy", None, None))
    return jax.shard_map(
        on_device,
        mesh=mesh,
        in_specs=placed,
        out_specs=(P("copy", "dp", None), P("copy")),
        check_vma=False,
    )
```

time: 1190 us -> 120 us (0.10)
  waiting for transfers between devices: 730 us -> 0 us
  blocking collectives: 332 us -> 0 us
  Pallas kernels: 0 us -> 115 us
  other arithmetic: 45.3 us -> 0.68 us
  local copies, waits for them, and re-layouts: 42.2 us -> 3.39 us
  matrix products: 20.4 us -> 0 us
  between operations: 17.2 us -> 0.64 us
    unnamed x2 -> x0, waiting for transfers between devices: 647 us -> none
    psum x1 -> x0, blocking collectives: 332 us -> none  [on_device(): square_sum = lax.psum(jnp.sum(grad_rows * grad_rows), 'dp')]
    pallas_call x0 -> x1, Pallas kernels: none -> 115 us  [on_device(): pl.pallas_call(kernel, out_shape=(jax.ShapeDtypeStruct((8, CLASSES), F32)...]
    ppermute x1 -> x0, waiting for transfers between devices: 83.3 us -> none  [from_partner(): return lax.ppermute(value, axis, pairs)]
    unnamed x14 -> x1, local copies, waits for them, and re-layouts: 42.2 us -> 1.59 us
    reduce_sum x5 -> x0, other arithmetic: 25.6 us -> none  [the longest x1 10.1 us: on_device(): wnorm = jnp.sqrt(jnp.sum(wide_f * wide_f))]
    dot_general x2 -> x0, matrix products: 20.4 us -> none  [the longest x1 13.3 us: on_device(): lax.dot_general(feats, grad_logits, (((0,), (0,)), ((), ())), preferred_e...]
    convert_element_type x2 -> x1, other arithmetic: 15.6 us -> 0.68 us  [on_device(): lab = jnp.broadcast_to(labels.astype(F32)[None, :], (8, IMG))]
  transfers between devices with their start and end apart: 2 -> 0, of which waited for: 2 -> 0; matrix products, arithmetic and copies ran while one was open for 4% -> 0% of each run, Pallas kernels for 0% -> 0%
where the time goes in v1:
time: 120 us
  Pallas kernels  115 us (96%)
  local copies, waits for them, and re-layouts  3.39 us (3%)
    pallas_call x1, Pallas kernels, on_device(): pl.pallas_call(kernel, out_shape=(jax.ShapeDtypeStruct((8, CLASSES), F32)...  115 us

profile of v1, /device:TPU:1, one launch (start us, length us, event | category | flops | bytes accessed | tf_op | source)
XLA Modules:
  0.0 119.9 jit_solution(13908519713693683100)
XLA Ops:
  0.6 0.7 convert_element_type.3
  1.3 0.6 broadcast_in_dim.4.lab_in
  1.9 115.2 %shard_map.50 = (f32[8,5120]{1,0:T(8,128)}, f32[8,128]{1,0:T(8,128)}) custom-call(bf16[384,1024]{1,0:T(8,128)(2,1)} %bitcast.5, bf16[1024,5120]{1,0:T(8,128)(2,1)} %bitcast.4, f32[8,384]{1,0:T(8,128)} %broadcast_in_dim.4.lab_in), custom_call_target="tpu_custom_call" | custom-call | tf_op jit(solution)/shard_map/pallas_call | solution.py:541
  117.1 1.2 slice.3
  118.3 1.6 %copy.6 = f32[1,8,5120]{2,1,0:T(8,128)} copy(f32[1,8,5120]{2,1,0:T(8,128)} %bitcast.6) | data formatting | bytes 327680

commit v2 on v1

--- a/solution.py
+++ b/solution.py
@@ -2,6 +2,7 @@
 
 import jax
 import jax.numpy as jnp
+import numpy as np
 from jax import lax
 from jax.experimental import pallas as pl
 from jax.experimental.pallas import tpu as pltpu
@@ -16,9 +17,11 @@
 IMAGES = 49152
 HALF = IMG // 2
 GI = 2 * IMG
+HALF_LOG2E = 0.5 * float(np.log2(np.e))
 trust = 32.0
 decay = 5e-05
 F32, BF16 = jnp.float32, jnp.bfloat16
+STREAMS = ((1, True, 0, 256), (1, True, 256, SL), (0, False, 0, 384), (0, True, 384, SL))
 
 
 def fold_lanes(v):
@@ -38,12 +41,11 @@
 def kernel(
     f_in, w_in, lab_in,
     out_ref, loss_ref,
-    F, FT, WS, W16, LAB, LABC, X, G, ACC, STR, COLT, LA, LS, TB, GB,
+    LROW, F, FT, WS, W16, LAB, LABC, X, G, ACC, STR, COLT, LA, LS, TB, GB,
     SCZ, SCY, SCX,
-    S00, R00, S01, R01, S10, R10, S11, R11,
+    bufs,
     loc_sem, fs, fr, ws, wr, ls, lr, ss, sr, as_, ar,
     zs, zr, ys, yr, xs, xr,
-    s00s, s00r, s01s, s01r, s10s, s10r, s11s, s11r,
 ):
     cp = lax.axis_index("copy")
     dp = lax.axis_index("dp")
@@ -82,6 +84,7 @@
         return pl.ds(pl.multiple_of(((c * 2 + h) * 2 + k) * SL, 128), SL)
 
     my_s = slice_of(cp, xh, core)
+    base = ((cp * 2 + xh) * 2 + core) * SL
 
     def block(h, k, lo, rows):
         return pl.ds(pl.multiple_of((h * 2 + k) * HALF + lo, 16), rows)
@@ -96,10 +99,11 @@
         pltpu.make_async_copy(
             w_in.at[pl.ds(pl.multiple_of((dp // 2) * 16, 16), 16), :], W16, loc_sem.at[3]
         ),
-        pltpu.make_async_copy(lab_in, LAB.at[xh, core], loc_sem.at[4]),
     ]
     for c in loc:
         c.start()
+    LROW[...] = jnp.broadcast_to(lab_in[...].astype(F32), (8, IMG))
+    LAB[xh, core] = LROW[...]
 
     peers = [peer(g) for g in group] + [ypeer(o) for o in range(1, NY)] + [zpeer(o) for o in range(1, NZ)]
     barrier = pltpu.get_barrier_semaphore()
@@ -182,7 +186,7 @@
 
     lab_kinds = [(0, 0, 1), (0, 1, 0), (0, 1, 1)]
     for n, g in enumerate(lab_kinds):
-        push(lab_in, LAB.at[xh, core], ls.at[n], lr.at[n], peer(g))
+        push(LROW, LAB.at[xh, core], ls.at[n], lr.at[n], peer(g))
 
     def logits(i, b, h):
         rows = pl.ds(pl.multiple_of(h * IMG, 128), IMG)
@@ -190,17 +194,21 @@
 
         def body(t, carry):
             at = pl.ds(pl.multiple_of(h * IMG + t * 128, 128), 128)
-            lg = X[i, b, at, :]
-            m = jnp.max(lg, axis=1, keepdims=True)
-            e = jnp.exp(0.5 * (lg - m))
-            s = jnp.sum(e, axis=1, keepdims=True)
-            s2 = jnp.sum(e * e, axis=1, keepdims=True)
+            lg = [X[i, b, at, k * 128 : k * 128 + 128] for k in range(SL // 128)]
+            m = jnp.max(functools.reduce(jnp.maximum, lg), axis=1, keepdims=True)
+            s = s2 = 0.0
+            for v in lg:
+                e = jnp.exp2((v - m) * HALF_LOG2E)
+                s = s + e
+                s2 = s2 + e * e
+            s = jnp.sum(s, axis=1, keepdims=True)
+            s2 = jnp.sum(s2, axis=1, keepdims=True)
             lane = lax.broadcasted_iota(jnp.int32, (128, 128), 1)
             tile = jnp.where(lane == 0, m, jnp.where(lane == 1, s, s2))
             STR[0, b, 4 * i : 4 * i + 4, at] = tile.T[0:4]
             return carry
 
-        lax.fori_loop(0, IMG // 128, body, 0)
+        lax.fori_loop(0, IMG // 128, body, 0, unroll=True)
 
     def transpose(i, b, h):
         def body(t, carry):
@@ -228,7 +236,7 @@
                 )
                 for b in range(2):
                     o = (h * 2 + k) * HALF
-                    LABC[b, o : o + HALF, :] = rows[b * HALF : b * HALF + HALF]
+                    LABC[b, o : o + HALF, :] = rows[b * HALF : b * HALF + HALF] - base.astype(F32)
 
     def send_stats(b):
         for n, g in enumerate(group):
@@ -237,8 +245,6 @@
     def wait_stats(b):
         for n, g in enumerate(group):
             arrive(STR.at[slot(g), b], ss.at[b, n], sr.at[b, n])
-
-    base = ((cp * 2 + xh) * 2 + core) * SL
 
     def combine(b):
         rows = []
@@ -261,7 +267,7 @@
                 ),
                 (8, 128),
             )
-            rows += [m, 1.0 / s, 1.0 / s2]
+            rows += [m, 1.0 / s, 0.5 / s2]
         pack = jnp.concatenate(rows + rows[:2], axis=0)
         for k in range(GI // 128):
             part = pack[:, k * 128 : (k + 1) * 128]
@@ -274,23 +280,29 @@
         def body(t, carry):
             at = pl.ds(pl.multiple_of(t * R, R), R)
             c = COLT[at, :]
-            cls = (lax.broadcasted_iota(jnp.int32, (R, SL), 1) + base).astype(F32)
-            oh = cls == LABC[b, at, 0:1]
-            x0 = X[0, b, at, :] - c[:, 0:1]
-            x1 = X[1, b, at, :] - c[:, 3:4]
-            e0 = jnp.exp(0.5 * x0)
-            e1 = jnp.exp(0.5 * x1)
-            s0 = e0 * c[:, 1:2]
-            s1 = e1 * c[:, 4:5]
-            q0 = s0.astype(BF16).astype(F32)
-            q1 = s1.astype(BF16).astype(F32)
-            p0 = e0 * e0 * c[:, 2:3]
-            p1 = e1 * e1 * c[:, 5:6]
-            hot = jnp.where(oh, 0.5, 0.0)
-            G[0, at, :] = (0.5 * p0 - hot + (s0 - q1)).astype(BF16)
-            G[1, at, :] = (0.5 * p1 - hot + (s1 - q0)).astype(BF16)
-            l0 = fold_lanes((q1 + hot) * x0) - c[:, 0:1] * fold_lanes(s1 - q1)
-            l1 = fold_lanes((q0 + hot) * x1) - c[:, 3:4] * fold_lanes(s0 - q0)
+            m0, r0, k0, m1, r1, k1 = (jnp.broadcast_to(c[:, j : j + 1], (R, 128)) for j in range(6))
+            lab = jnp.broadcast_to(LABC[b, at, 0:1], (R, 128))
+            lane = lax.broadcasted_iota(jnp.int32, (R, 128), 1).astype(F32)
+            l0 = l1 = d0 = d1 = 0.0
+            for k in range(SL // 128):
+                ln = slice(k * 128, k * 128 + 128)
+                x0 = X[0, b, at, ln] - m0
+                x1 = X[1, b, at, ln] - m1
+                e0 = jnp.exp2(x0 * HALF_LOG2E)
+                e1 = jnp.exp2(x1 * HALF_LOG2E)
+                s0 = e0 * r0
+                s1 = e1 * r1
+                q0 = s0.astype(BF16).astype(F32)
+                q1 = s1.astype(BF16).astype(F32)
+                hot = jnp.where(lane == lab - float(k * 128), 0.5, 0.0)
+                G[0, at, ln] = (e0 * e0 * k0 - hot + (s0 - q1)).astype(BF16)
+                G[1, at, ln] = (e1 * e1 * k1 - hot + (s1 - q0)).astype(BF16)
+                l0 = l0 + (q1 + hot) * x0
+                l1 = l1 + (q0 + hot) * x1
+                d0 = d0 + (s0 - q0)
+                d1 = d1 + (s1 - q1)
+            l0 = l0 - m0 * d1
+            l1 = l1 - m1 * d0
             LA[0, :, :] = LA[0] + fold_rows(l0)
             LA[1, :, :] = LA[1] + fold_rows(l1)
             return carry
@@ -402,70 +414,109 @@
         for way in range(2):
             arrive(RB[steps - 1].at[way], ssem.at[way, steps - 1], rsem.at[way, steps - 1])
 
-    ydirs, zdirs = (ypeer(NY - 1), ypeer(1)), (zpeer(NZ - 1), zpeer(1))
-
-    def acc_chunk(i, size):
+    c0, c1 = D // NZ, D // NY
+
+    def plain(i, size, cols):
         def chunk(j, lo, rows):
-            return ACC[i, pl.ds(pl.multiple_of(j * size + lo, 16), rows), :]
+            return ACC[i, pl.ds(pl.multiple_of(j * size + lo, 16), rows), cols]
 
         return chunk
 
-    c0, c1 = D // NZ, D // NY
-    r0 = ring(NZ, z, c0 // 2, acc_chunk(0, c0), S00, R00, s00s, s00r, zdirs)
-    r1 = ring(NY, y, c1 // 2, acc_chunk(1, c1), S10, R10, s10s, s10r, ydirs)
-
-    def own0():
-        at = pl.ds(pl.multiple_of(z * c0, 16), c0)
-        ACC[0, at, :] = ACC[0, at, :] + (R00[-1][0].astype(F32) + R00[-1][1].astype(F32))
-
-    def own1():
-        at = pl.ds(pl.multiple_of(y * c1, 16), c1)
-        ACC[1, at, :] = ACC[1, at, :] + (R10[-1][0].astype(F32) + R10[-1][1].astype(F32))
-
-    def sub_chunk(i, first):
+    def strided(i, cols):
         def chunk(j, lo, rows):
-            return ACC[i, pl.ds(pl.multiple_of(first + j * 32 + lo, 16), rows), :]
+            return jnp.concatenate(
+                [
+                    ACC[i, pl.ds(pl.multiple_of((zz * NY + j) * 32, 32), 32), cols]
+                    for zz in range(lo // 32, (lo + rows) // 32)
+                ],
+                axis=0,
+            )
 
         return chunk
 
-    q0 = ring(NY, y, 16, sub_chunk(0, z * c0), S01, R01, s01s, s01r, ydirs)
-    q1 = ring(NZ, z, 16, sub_chunk(1, y * c1), S11, R11, s11s, s11r, zdirs)
-
-    def go(gen):
-        for _ in gen:
-            return
-
+    def of_result(ref):
+        def chunk(j, lo, rows):
+            return ref[pl.ds(pl.multiple_of(j * 32 + lo, 16), rows), :]
+
+        return chunk
+
+    inv = 1.0 / IMAGES
+    sq = [0.0, 0.0]
+
+    class Stream:
+        def __init__(self, n):
+            self.role, y_first, lo, hi = STREAMS[n]
+            self.cols = slice(lo, hi)
+            buf = bufs[n]
+            self.res, (s1, r1), (s2, r2) = buf["res"], buf["first"], buf["second"]
+            sems1, sems2 = buf["sems"]
+            ydirs, zdirs = (ypeer(NY - 1), ypeer(1)), (zpeer(NZ - 1), zpeer(1))
+            first = (NY, y, ydirs) if y_first else (NZ, z, zdirs)
+            second = (NZ, z, zdirs) if y_first else (NY, y, ydirs)
+            self.size, self.me1, self.me2 = D // first[0], first[1], second[1]
+            if y_first and self.role == 0:
+                self.chunk = strided(0, self.cols)
+            else:
+                self.chunk = plain(self.role, self.size, self.cols)
+            self.r1, self.r2 = r1, r2
+            self.a = ring(first[0], first[1], self.size // 2, self.chunk, s1, r1, *sems1, first[2])
+            self.b = ring(second[0], second[1], 16, of_result(self.res), s2, r2, *sems2, second[2])
+
+        def one(self):
+            next(self.a, None)
+
+        def turn(self):
+            next(self.a, None)
+            own = self.chunk(self.me1, 0, self.size)
+            self.res[...] = own + (self.r1[-1][0].astype(F32) + self.r1[-1][1].astype(F32))
+            next(self.b, None)
+
+        def two(self):
+            next(self.b, None)
+
+        def end(self):
+            next(self.b, None)
+            at = pl.ds(pl.multiple_of(self.me2 * 32, 32), 32)
+            v = (self.res[at, :] + (self.r2[-1][0].astype(F32) + self.r2[-1][1].astype(F32))) * inv
+            TB[self.role, :, self.cols] = v
+            q = v * v
+            for k in range(v.shape[1] // 128):
+                sq[self.role] = sq[self.role] + fold_rows(q[:, k * 128 : k * 128 + 128])
+
+    A1, A2, B1, B2 = (Stream(n) for n in range(4))
+    wgrad(1, 1, y + NY // 2, 1, c1, False)
+    A1.one()
+    A2.one()
     wgrad(0, 1, z + NZ // 2, 1, c0, False)
-    wgrad(1, 1, y + NY // 2, 1, c1, False)
-    go(r0)
-    go(r1)
+    B1.one()
+    wgrad(1, 1, y + NY // 2 + 1, NY - 1, c1, False)
+    A1.one()
     wgrad(0, 1, z + NZ // 2 + 1, NZ - 1, c0, False)
-    go(r0)
-    wgrad(1, 1, y + NY // 2 + 1, NY - 1, c1, False)
-    go(r1)
-    go(r0)
-    go(r0)
-    go(r1)
-    own1()
-    go(q1)
-    go(r0)
-    own0()
-    go(q0)
-    go(q1)
-    go(q0)
-    go(q1)
-    go(q0)
-    go(q1)
-    go(q1)
-
-    inv = 1.0 / IMAGES
-    sq = []
-    for i in range(2):
-        at = pl.ds(pl.multiple_of(z * c0 + y * 32 if i == 0 else y * c1 + z * 32, 32), 32)
-        last = (R01 if i == 0 else R11)[-1]
-        v = (ACC[i, at, :] + (last[0].astype(F32) + last[1].astype(F32))) * inv
-        TB[i, :, :] = v
-        sq.append(fold_rows(fold_lanes(v * v)))
+    B1.one()
+    B2.one()
+    A2.one()
+    B1.one()
+    A1.turn()
+    B1.one()
+    B2.one()
+    A1.two()
+    A2.turn()
+    A1.two()
+    B1.turn()
+    A1.two()
+    A2.two()
+    B1.two()
+    B2.turn()
+    A1.end()
+    A2.two()
+    B1.end()
+    B2.two()
+    A2.two()
+    B2.two()
+    A2.end()
+    B2.two()
+    B2.end()
+
     for n, g in enumerate(group):
         a, b, c = g
         off = pl.ds(pl.multiple_of((flip(xh, b) * 2 + flip(core, c)) * 8, 8), 8)
@@ -509,7 +560,7 @@
     gnorm = jnp.sqrt(mine[0:1])
     wnorm = jnp.sqrt(mine[2:3])
     scale = trust * wnorm / (gnorm + decay * wnorm)
-    loss_ref[...] = jnp.broadcast_to(mine[1:2] * inv, (8, 128))
+    loss_ref[0] = jnp.sum(mine[1:2]) * inv
 
     for n, (a, b, c) in enumerate(group):
         src = slice_of(flip(cp, a), flip(xh, b), flip(core, c))
@@ -523,30 +574,38 @@
 
 
 def on_device(features, labels, weight):
-    lab = jnp.broadcast_to(labels.astype(F32)[None, :], (8, IMG))
+    lab = labels[None, :]
     dma = pltpu.SemaphoreType.DMA
     vm = pltpu.VMEM
     any_ = pl.BlockSpec(memory_space=pl.ANY)
-    ring_bufs = []
-    ring_sems = []
-    for rows, types in (
-        (D // NZ, [BF16] * (NZ // 2 - 1) + [F32]),
-        (32, [F32] * (NY // 2)),
-        (D // NY, [BF16] * (NY // 2)),
-        (32, [F32] * (NZ // 2)),
-    ):
-        bufs = tuple(vm((2, rows // 2 if t == 0 else rows, SL), dt) for t, dt in enumerate(types))
-        ring_bufs += [bufs, bufs]
-        ring_sems += [dma((2, len(types)))] * 2
+    def buffers(rows, width, types):
+        one = tuple(vm((2, rows // 2 if t == 0 else rows, width), dt) for t, dt in enumerate(types))
+        return (one, one)
+
+    bufs = []
+    for _, y_first, lo, hi in STREAMS:
+        if y_first:
+            n1, n2, types = NY, NZ, [BF16] * (NY // 2)
+        else:
+            n1, n2, types = NZ, NY, [BF16] * (NZ // 2 - 1) + [F32]
+        bufs.append(
+            dict(
+                res=vm((D // n1, hi - lo), F32),
+                first=buffers(D // n1, hi - lo, types),
+                second=buffers(32, hi - lo, [F32] * (n2 // 2)),
+                sems=((dma((2, n1 // 2)), dma((2, n1 // 2))), (dma((2, n2 // 2)), dma((2, n2 // 2)))),
+            )
+        )
     update, loss = pl.pallas_call(
         kernel,
         out_shape=(
             jax.ShapeDtypeStruct((8, CLASSES), F32),
-            jax.ShapeDtypeStruct((8, 128), F32),
+            jax.ShapeDtypeStruct((1,), F32),
         ),
-        in_specs=[any_, any_, any_],
-        out_specs=(pl.BlockSpec(memory_space=vm), pl.BlockSpec(memory_space=vm)),
+        in_specs=[any_, any_, pl.BlockSpec(memory_space=vm)],
+        out_specs=(pl.BlockSpec(memory_space=vm), pl.BlockSpec(memory_space=pltpu.SMEM)),
         scratch_shapes=[
+            vm((8, IMG), F32),
             vm((2, 2, GI, D), BF16),
             vm((2, 2, D, GI), BF16),
             vm((2, D, SL), BF16),
@@ -565,8 +624,8 @@
             vm((NZ, 8, 128), F32),
             vm((NY, 8, 128), F32),
             vm((8, 8, 128), F32),
-            *ring_bufs,
-            dma((5,)),
+            bufs,
+            dma((4,)),
             dma((2, 13)), dma((2, 13)),
             dma((8,)), dma((8,)),
             dma((3,)), dma((3,)),
@@ -575,13 +634,12 @@
             dma((NZ - 1,)), dma((NZ - 1,)),
             dma((NY - 1,)), dma((NY - 1,)),
             dma((7,)), dma((7,)),
-            *ring_sems,
         ],
         compiler_params=pltpu.CompilerParams(
             collective_id=0, has_side_effects=True, vmem_limit_bytes=56 * 2**20
         ),
     )(features[0], weight[0], lab)
-    return (update[None], loss[0, :1])
+    return (update[None], loss)
 
 
 def solution(mesh):

time: 120 us -> 123 us (1.025)
  Pallas kernels: 115 us -> 117 us
  between operations: 0.64 us -> 2.4 us
    pallas_call x1, Pallas kernels: 115 us -> 117 us  [on_device(): pl.pallas_call(kernel, out_shape=(jax.ShapeDtypeStruct((8, CLASSES), F32)...]
where the time goes in v2:
time: 123 us; the launch traced here: 122 us
  Pallas kernels  117 us (95%)
  local copies, waits for them, and re-layouts  2.84 us (2%)
  between operations  2.4 us (2%)
    pallas_call x1, Pallas kernels, on_device(): pl.pallas_call(kernel, out_shape=(jax.ShapeDtypeStruct((8, CLASSES), F32)...  117 us

profile of v2, /device:TPU:1, one launch (start us, length us, event | category | flops | bytes accessed | tf_op | source)
XLA Modules:
  0.0 122.4 jit_solution(2194760356490972979)
XLA Ops:
  0.6 1.2 %broadcast_in_dim.6.lab_in = s32[1,384]{1,0:T(1,128)} reshape(s32[384]{0:T(512)} %param.4) | data formatting | bytes 3072 | tf_op jit(solution)/shard_map/broadcast_in_dim | solution.py:577
  1.9 117.1 %shard_map.50 = (f32[8,5120]{1,0:T(8,128)}, f32[1]{0:T(128)}) custom-call(bf16[384,1024]{1,0:T(8,128)(2,1)} %bitcast.4, bf16[1024,5120]{1,0:T(8,128)(2,1)} %bitcast.3, s32[1,384]{1,0:T(1,128)} %broadcast_in_dim.6.lab_in), custom_call_target="tpu_custom_call" | custom-call | tf_op jit(solution)/shard_map/pallas_call | solution.py:599
  119.0 1.6 %copy.7 = f32[1,8,5120]{2,1,0:T(8,128)} copy(f32[1,8,5120]{2,1,0:T(8,128)} %bitcast.5) | data formatting | bytes 327680

commit v3 on v1

--- a/solution.py
+++ b/solution.py
@@ -2,6 +2,7 @@
 
 import jax
 import jax.numpy as jnp
+import numpy as np
 from jax import lax
 from jax.experimental import pallas as pl
 from jax.experimental.pallas import tpu as pltpu
@@ -16,6 +17,7 @@
 IMAGES = 49152
 HALF = IMG // 2
 GI = 2 * IMG
+HALF_LOG2E = 0.5 * float(np.log2(np.e))
 trust = 32.0
 decay = 5e-05
 F32, BF16 = jnp.float32, jnp.bfloat16
@@ -82,6 +84,7 @@
         return pl.ds(pl.multiple_of(((c * 2 + h) * 2 + k) * SL, 128), SL)
 
     my_s = slice_of(cp, xh, core)
+    base = ((cp * 2 + xh) * 2 + core) * SL
 
     def block(h, k, lo, rows):
         return pl.ds(pl.multiple_of((h * 2 + k) * HALF + lo, 16), rows)
@@ -190,17 +193,21 @@
 
         def body(t, carry):
             at = pl.ds(pl.multiple_of(h * IMG + t * 128, 128), 128)
-            lg = X[i, b, at, :]
-            m = jnp.max(lg, axis=1, keepdims=True)
-            e = jnp.exp(0.5 * (lg - m))
-            s = jnp.sum(e, axis=1, keepdims=True)
-            s2 = jnp.sum(e * e, axis=1, keepdims=True)
+            lg = [X[i, b, at, k * 128 : k * 128 + 128] for k in range(SL // 128)]
+            m = jnp.max(functools.reduce(jnp.maximum, lg), axis=1, keepdims=True)
+            s = s2 = 0.0
+            for v in lg:
+                e = jnp.exp2((v - m) * HALF_LOG2E)
+                s = s + e
+                s2 = s2 + e * e
+            s = jnp.sum(s, axis=1, keepdims=True)
+            s2 = jnp.sum(s2, axis=1, keepdims=True)
             lane = lax.broadcasted_iota(jnp.int32, (128, 128), 1)
             tile = jnp.where(lane == 0, m, jnp.where(lane == 1, s, s2))
             STR[0, b, 4 * i : 4 * i + 4, at] = tile.T[0:4]
             return carry
 
-        lax.fori_loop(0, IMG // 128, body, 0)
+        lax.fori_loop(0, IMG // 128, body, 0, unroll=True)
 
     def transpose(i, b, h):
         def body(t, carry):
@@ -228,7 +235,7 @@
                 )
                 for b in range(2):
                     o = (h * 2 + k) * HALF
-                    LABC[b, o : o + HALF, :] = rows[b * HALF : b * HALF + HALF]
+                    LABC[b, o : o + HALF, :] = rows[b * HALF : b * HALF + HALF] - base.astype(F32)
 
     def send_stats(b):
         for n, g in enumerate(group):
@@ -237,9 +244,6 @@
     def wait_stats(b):
         for n, g in enumerate(group):
             arrive(STR.at[slot(g), b], ss.at[b, n], sr.at[b, n])
-
-    base = ((cp * 2 + xh) * 2 + core) * SL
-
     def combine(b):
         rows = []
         for i in range(2):
@@ -261,7 +265,7 @@
                 ),
                 (8, 128),
             )
-            rows += [m, 1.0 / s, 1.0 / s2]
+            rows += [m, 1.0 / s, 0.5 / s2]
         pack = jnp.concatenate(rows + rows[:2], axis=0)
         for k in range(GI // 128):
             part = pack[:, k * 128 : (k + 1) * 128]
@@ -274,23 +278,29 @@
         def body(t, carry):
             at = pl.ds(pl.multiple_of(t * R, R), R)
             c = COLT[at, :]
-            cls = (lax.broadcasted_iota(jnp.int32, (R, SL), 1) + base).astype(F32)
-            oh = cls == LABC[b, at, 0:1]
-            x0 = X[0, b, at, :] - c[:, 0:1]
-            x1 = X[1, b, at, :] - c[:, 3:4]
-            e0 = jnp.exp(0.5 * x0)
-            e1 = jnp.exp(0.5 * x1)
-            s0 = e0 * c[:, 1:2]
-            s1 = e1 * c[:, 4:5]
-            q0 = s0.astype(BF16).astype(F32)
-            q1 = s1.astype(BF16).astype(F32)
-            p0 = e0 * e0 * c[:, 2:3]
-            p1 = e1 * e1 * c[:, 5:6]
-            hot = jnp.where(oh, 0.5, 0.0)
-            G[0, at, :] = (0.5 * p0 - hot + (s0 - q1)).astype(BF16)
-            G[1, at, :] = (0.5 * p1 - hot + (s1 - q0)).astype(BF16)
-            l0 = fold_lanes((q1 + hot) * x0) - c[:, 0:1] * fold_lanes(s1 - q1)
-            l1 = fold_lanes((q0 + hot) * x1) - c[:, 3:4] * fold_lanes(s0 - q0)
+            m0, r0, k0, m1, r1, k1 = (jnp.broadcast_to(c[:, j : j + 1], (R, 128)) for j in range(6))
+            lab = jnp.broadcast_to(LABC[b, at, 0:1], (R, 128))
+            lane = lax.broadcasted_iota(jnp.int32, (R, 128), 1).astype(F32)
+            l0 = l1 = d0 = d1 = 0.0
+            for k in range(SL // 128):
+                ln = slice(k * 128, k * 128 + 128)
+                x0 = X[0, b, at, ln] - m0
+                x1 = X[1, b, at, ln] - m1
+                e0 = jnp.exp2(x0 * HALF_LOG2E)
+                e1 = jnp.exp2(x1 * HALF_LOG2E)
+                s0 = e0 * r0
+                s1 = e1 * r1
+                q0 = s0.astype(BF16).astype(F32)
+                q1 = s1.astype(BF16).astype(F32)
+                hot = jnp.where(lane == lab - float(k * 128), 0.5, 0.0)
+                G[0, at, ln] = (e0 * e0 * k0 - hot + (s0 - q1)).astype(BF16)
+                G[1, at, ln] = (e1 * e1 * k1 - hot + (s1 - q0)).astype(BF16)
+                l0 = l0 + (q1 + hot) * x0
+                l1 = l1 + (q0 + hot) * x1
+                d0 = d0 + (s0 - q0)
+                d1 = d1 + (s1 - q1)
+            l0 = l0 - m0 * d1
+            l1 = l1 - m1 * d0
             LA[0, :, :] = LA[0] + fold_rows(l0)
             LA[1, :, :] = LA[1] + fold_rows(l1)
             return carry
@@ -361,8 +371,8 @@
     combine(0)
     finish(0)
     share_rest(1)
-    wgrad(0, 0, 0, 4, D // 4, True)
-    wgrad(1, 0, 0, 4, D // 4, True)
+    wgrad(0, 0, 0, 1, D, True)
+    wgrad(1, 0, 0, 1, D, True)
     shared_neighbours(1)
     logits(1, 1, 0)
     logits(1, 1, 1)
@@ -439,6 +449,24 @@
     wgrad(1, 1, y + NY // 2, 1, c1, False)
     go(r0)
     go(r1)
+
+    row = lax.broadcasted_iota(jnp.int32, (8, 128), 0)
+
+    def put_rows(tile, r, v):
+        tile = jnp.where(row == r, jnp.where(cp == 0, v[0], v[1]), tile)
+        return jnp.where(row == 3 + r, jnp.where(cp == 0, v[1], v[0]), tile)
+
+    lsums, wsums = [], []
+    for i in range(2):
+        wq = 0.0
+        for h in range(2):
+            at = pl.ds(pl.multiple_of(h * 512 + z * 64 + y * 16, 16), 16)
+            wv = WS[i, at, :].astype(F32)
+            wq = wq + fold_rows(fold_lanes(wv * wv))
+        wsums.append(jnp.sum(wq, axis=0, keepdims=True))
+        lsums.append(jnp.sum(LS[i] * 0.125 - LA[i], axis=0, keepdims=True))
+    tile = put_rows(put_rows(jnp.zeros((8, 128), F32), 1, lsums), 2, wsums)
+
     wgrad(0, 1, z + NZ // 2 + 1, NZ - 1, c0, False)
     go(r0)
     wgrad(1, 1, y + NY // 2 + 1, NY - 1, c1, False)
@@ -466,31 +494,15 @@
         v = (ACC[i, at, :] + (last[0].astype(F32) + last[1].astype(F32))) * inv
         TB[i, :, :] = v
         sq.append(fold_rows(fold_lanes(v * v)))
+    tile = put_rows(tile, 0, [jnp.sum(v, axis=0, keepdims=True) for v in sq])
+    SCZ[0, :, :] = tile
+    for o in range(1, NZ):
+        push(SCZ.at[0], SCZ.at[o], zs.at[o - 1], zr.at[o - 1], zpeer(o))
     for n, g in enumerate(group):
         a, b, c = g
         off = pl.ds(pl.multiple_of((flip(xh, b) * 2 + flip(core, c)) * 8, 8), 8)
         push(TB.at[a, off], GB.at[:, my_s], as_.at[n], ar.at[n], peer(g))
     GB[:, my_s] = TB[0, pl.ds(pl.multiple_of((xh * 2 + core) * 8, 8), 8), :]
-
-    vals = []
-    for i in range(2):
-        wq = 0.0
-        for h in range(2):
-            at = pl.ds(pl.multiple_of(((h * NZ + z) * NY + y) * 16, 16), 16)
-            wv = WS[i, at, :].astype(F32)
-            wq = wq + fold_rows(fold_lanes(wv * wv))
-        lv = LS[i] * 0.125 - LA[i]
-        vals.append([jnp.sum(v, axis=0, keepdims=True) for v in (sq[i], lv, wq)])
-    row = lax.broadcasted_iota(jnp.int32, (8, 128), 0)
-    tile = jnp.zeros((8, 128), F32)
-    for r in range(3):
-        v0, v1 = vals[0][r], vals[1][r]
-        tile = jnp.where(row == r, jnp.where(cp == 0, v0, v1), tile)
-        tile = jnp.where(row == 3 + r, jnp.where(cp == 0, v1, v0), tile)
-
-    SCZ[0, :, :] = tile
-    for o in range(1, NZ):
-        push(SCZ.at[0], SCZ.at[o], zs.at[o - 1], zr.at[o - 1], zpeer(o))
     for o in range(1, NZ):
         arrive(SCZ.at[o], zs.at[o - 1], zr.at[o - 1])
     SCY[0, :, :] = jnp.sum(SCZ[...], axis=0)

time: 120 us -> 116 us (0.967)
  Pallas kernels: 115 us -> 111 us
    pallas_call x1, Pallas kernels: 115 us -> 111 us  [on_device(): pl.pallas_call(kernel, out_shape=(jax.ShapeDtypeStruct((8, CLASSES), F32)...]
where the time goes in v3:
time: 116 us
  Pallas kernels  111 us (96%)
  local copies, waits for them, and re-layouts  3.39 us (3%)
    pallas_call x1, Pallas kernels, on_device(): pl.pallas_call(kernel, out_shape=(jax.ShapeDtypeStruct((8, CLASSES), F32)...  111 us

profile of v3, /device:TPU:1, one launch (start us, length us, event | category | flops | bytes accessed | tf_op | source)
XLA Modules:
  0.0 116.0 jit_solution(1440807461862201735)
XLA Ops:
  0.6 0.7 convert_element_type.3
  1.3 0.6 broadcast_in_dim.4.lab_in
  1.9 111.3 %shard_map.50 = (f32[8,5120]{1,0:T(8,128)}, f32[8,128]{1,0:T(8,128)}) custom-call(bf16[384,1024]{1,0:T(8,128)(2,1)} %bitcast.5, bf16[1024,5120]{1,0:T(8,128)(2,1)} %bitcast.4, f32[8,384]{1,0:T(8,128)} %broadcast_in_dim.4.lab_in), custom_call_target="tpu_custom_call" | custom-call | tf_op jit(solution)/shard_map/pallas_call | solution.py:553
  113.3 1.2 %slice.3 = f32[1,1]{1,0:T(1,128)} slice(f32[8,128]{1,0:T(8,128)} %get-tuple-element.5), slice={[0:1], [0:1]} | slice | bytes 8 | tf_op jit(solution)/shard_map/slice | solution.py:596
  114.4 1.6 %copy.6 = f32[1,8,5120]{2,1,0:T(8,128)} copy(f32[1,8,5120]{2,1,0:T(8,128)} %bitcast.6) | data formatting | bytes 327680

commit v4 on v3

--- a/solution.py
+++ b/solution.py
@@ -371,8 +371,6 @@
     combine(0)
     finish(0)
     share_rest(1)
-    wgrad(0, 0, 0, 1, D, True)
-    wgrad(1, 0, 0, 1, D, True)
     shared_neighbours(1)
     logits(1, 1, 0)
     logits(1, 1, 1)
@@ -383,6 +381,8 @@
     logits(0, 1, ox)
     send_stats(1)
     transpose(0, 1, ox)
+    wgrad(0, 0, 0, 1, D, True)
+    wgrad(1, 0, 0, 1, D, True)
     wait_stats(1)
     combine(1)
     finish(1)

time: 116 us -> 115 us (level)
    pallas_call x1, Pallas kernels: 111 us -> 110 us  [on_device(): pl.pallas_call(kernel, out_shape=(jax.ShapeDtypeStruct((8, CLASSES), F32)...]
where the time goes in v4:
time: 115 us
  Pallas kernels  110 us (96%)
  local copies, waits for them, and re-layouts  3.39 us (3%)
    pallas_call x1, Pallas kernels, on_device(): pl.pallas_call(kernel, out_shape=(jax.ShapeDtypeStruct((8, CLASSES), F32)...  110 us

profile of v4, /device:TPU:1, one launch (start us, length us, event | category | flops | bytes accessed | tf_op | source)
XLA Modules:
  0.0 114.6 jit_solution(16508779911043876455)
XLA Ops:
  0.6 0.7 convert_element_type.3
  1.3 0.6 broadcast_in_dim.4.lab_in
  1.9 109.8 %shard_map.50 = (f32[8,5120]{1,0:T(8,128)}, f32[8,128]{1,0:T(8,128)}) custom-call(bf16[384,1024]{1,0:T(8,128)(2,1)} %bitcast.5, bf16[1024,5120]{1,0:T(8,128)(2,1)} %bitcast.4, f32[8,384]{1,0:T(8,128)} %broadcast_in_dim.4.lab_in), custom_call_target="tpu_custom_call" | custom-call | tf_op jit(solution)/shard_map/pallas_call | solution.py:553
  111.8 1.2 %slice.3 = f32[1,1]{1,0:T(1,128)} slice(f32[8,128]{1,0:T(8,128)} %get-tuple-element.5), slice={[0:1], [0:1]} | slice | bytes 8 | tf_op jit(solution)/shard_map/slice | solution.py:596
  113.0 1.6 %copy.6 = f32[1,8,5120]{2,1,0:T(8,128)} copy(f32[1,8,5120]{2,1,0:T(8,128)} %bitcast.6) | data formatting | bytes 327680

commit v5 on v4

--- a/solution.py
+++ b/solution.py
@@ -446,8 +446,12 @@
             return
 
     wgrad(0, 1, z + NZ // 2, 1, c0, False)
+    go(r0)
     wgrad(1, 1, y + NY // 2, 1, c1, False)
+    go(r1)
+    wgrad(0, 1, z + NZ // 2 + 1, NZ - 1, c0, False)
     go(r0)
+    wgrad(1, 1, y + NY // 2 + 1, NY - 1, c1, False)
     go(r1)
 
     row = lax.broadcasted_iota(jnp.int32, (8, 128), 0)
@@ -467,10 +471,6 @@
         lsums.append(jnp.sum(LS[i] * 0.125 - LA[i], axis=0, keepdims=True))
     tile = put_rows(put_rows(jnp.zeros((8, 128), F32), 1, lsums), 2, wsums)
 
-    wgrad(0, 1, z + NZ // 2 + 1, NZ - 1, c0, False)
-    go(r0)
-    wgrad(1, 1, y + NY // 2 + 1, NY - 1, c1, False)
-    go(r1)
     go(r0)
     go(r0)
     go(r1)

time: 115 us -> 114 us (level)
  no operation moved by 1% of the time
where the time goes in v5:
time: 114 us
  Pallas kernels  110 us (96%)
  local copies, waits for them, and re-layouts  3.39 us (3%)
    pallas_call x1, Pallas kernels, on_device(): pl.pallas_call(kernel, out_shape=(jax.ShapeDtypeStruct((8, CLASSES), F32)...  110 us

profile of v5, /device:TPU:1, one launch (start us, length us, event | category | flops | bytes accessed | tf_op | source)
XLA Modules:
  0.0 114.2 jit_solution(13805805649867101130)
XLA Ops:
  0.6 0.7 convert_element_type.3
  1.3 0.6 broadcast_in_dim.4.lab_in
  1.9 109.5 %shard_map.50 = (f32[8,5120]{1,0:T(8,128)}, f32[8,128]{1,0:T(8,128)}) custom-call(bf16[384,1024]{1,0:T(8,128)(2,1)} %bitcast.5, bf16[1024,5120]{1,0:T(8,128)(2,1)} %bitcast.4, f32[8,384]{1,0:T(8,128)} %broadcast_in_dim.4.lab_in), custom_call_target="tpu_custom_call" | custom-call | tf_op jit(solution)/shard_map/pallas_call | solution.py:553
  111.5 1.2 %slice.3 = f32[1,1]{1,0:T(1,128)} slice(f32[8,128]{1,0:T(8,128)} %get-tuple-element.5), slice={[0:1], [0:1]} | slice | bytes 8 | tf_op jit(solution)/shard_map/slice | solution.py:596
  112.7 1.6 %copy.6 = f32[1,8,5120]{2,1,0:T(8,128)} copy(f32[1,8,5120]{2,1,0:T(8,128)} %bitcast.6) | data formatting | bytes 327680
